TPU v7x, 256 devices: a whole 4x4x8 slice. The times are simulated.
256 devices in a mesh: row: 32 (over y_lo, z, core), col: 8 (over x, y_hi).
Axes of the slice: x: 4, y: 4 (y_hi: 2, y_lo: 2; y = y_hi * 2 + y_lo), z: 8, core: 2. Of those that a mesh axis runs over, the one named last changes fastest.
Arguments:
- start_block: float32 [32768, 256], P(('row', 'col')), may hold values from -6 to 6
- tiles: bfloat16 [32, 8, 14, 128, 128], P('row', 'col'), may hold values from -0.125 to 0.125
- tile_rows: int32 [32, 8, 14], P('row', 'col'), may hold values from -1 to 255, as said below
- tile_cols: int32 [32, 8, 14], P('row', 'col'), may hold values from -1 to 255, as said below
- bounds: float32 [3], replicated, may hold values from -2.6 to 2.6, as said below
Outputs:
- filtered: float32 [32768, 256], P(('row', 'col'))
Inputs may be any that keep to these rules, and one draw needn't show every extreme that they name: Vector rows form blocks of 128 rows, one block a device, in row+col order. On the device at grid row r and grid column c, a live slot names a block row held by one of the devices (r, any column) and a block column held by one of the devices (any row, c). Live slots come first; each device has 1 to 14 live slots, and one device has exactly 14 in every draw. No block position is named twice, and the mirror of a named position is never named unless it lies on the diagonal. tile_rows and tile_cols are -1 together. `tile_cols`: same slots as tile_rows. bounds[0] < bounds[1] < bounds[2].
All inputs are finite; a program needn't handle non-finite values.
Results may differ from a plain program's by a relative error of at most 0.0042.
Values may be sent and summed in bfloat16 or wider, within the bound.
No kernel may reach another device: no remote copies, remote signals or barrier semaphores. Data moves between devices by JAX's collectives and lax.ppermute only.
A program may use at most 64 MiB of HBM per device.

v0:
```python
import jax
import jax.numpy as jnp
from jax import lax
from jax.sharding import PartitionSpec as P

DEGREE = 4


def local(start_block, tiles, tile_rows, tile_cols, bounds):
    rows_dev, vec_width = start_block.shape
    tile_size = tiles.shape[-1]
    blocks = rows_dev // tile_size
    row_count = lax.axis_size("row")
    col_count = lax.axis_size("col")
    near_count = col_count * blocks
    far_count = row_count * blocks
    row_index = lax.axis_index("row")
    slots = tiles.shape[2]
    tile_mats = tiles.reshape(slots, tile_size, tile_size)
    glob_rows = tile_rows.reshape(slots)
    glob_cols = tile_cols.reshape(slots)
    is_live = glob_rows >= 0
    local_rows = jnp.where(is_live, glob_rows - row_index * near_count, -1)
    local_cols = jnp.where(
        is_live, glob_cols // blocks // col_count * blocks + glob_cols % blocks, -1
    )
    row_table = (local_rows[None, :] == lax.iota(jnp.int32, near_count)[:, None]).astype(
        jnp.float32
    )
    col_table = (local_cols[None, :] == lax.iota(jnp.int32, far_count)[:, None]).astype(jnp.float32)
    rows_safe = jnp.maximum(local_rows, 0)
    cols_safe = jnp.maximum(local_cols, 0)

    def apply_matrix(vectors):
        low_vectors = vectors.astype(jnp.bfloat16)
        far_vectors = lax.all_gather(low_vectors, "row", axis=0, tiled=True).reshape(
            far_count, tile_size, vec_width
        )
        near_vectors = lax.all_gather(low_vectors, "col", axis=0, tiled=True).reshape(
            near_count, tile_size, vec_width
        )
        picked_far = jnp.take(far_vectors, cols_safe, axis=0)
        picked_near = jnp.take(near_vectors, rows_safe, axis=0)
        forward = jnp.einsum(
            "txy,tyk->txk", tile_mats, picked_far, preferred_element_type=jnp.float32
        )
        backward = jnp.einsum(
            "tyx,tyk->txk", tile_mats, picked_near, preferred_element_type=jnp.float32
        )
        near_partial = jnp.dot(
            row_table, forward.reshape(slots, -1), precision=lax.Precision.HIGHEST
        )
        far_partial = jnp.dot(
            col_table, backward.reshape(slots, -1), precision=lax.Precision.HIGHEST
        )
        mirrored = lax.psum_scatter(
            far_partial.reshape(far_count * tile_size, vec_width),
            "row",
            scatter_dimension=0,
            tiled=True,
        )
        combined = lax.psum_scatter(
            near_partial.reshape(near_count * tile_size, vec_width),
            "col",
            scatter_dimension=0,
            tiled=True,
        )
        return combined + mirrored

    half_width = (bounds[2] - bounds[1]) * 0.5
    center = (bounds[2] + bounds[1]) * 0.5
    sigma_one = half_width / (bounds[0] - center)
    previous = start_block
    current = (apply_matrix(start_block) - center * start_block) * (sigma_one / half_width)
    sigma = sigma_one
    for turn_index in range(DEGREE - 1):
        sigma_next = 1.0 / (2.0 / sigma_one - sigma)
        product = apply_matrix(current)
        following = (product - center * current) * (
            2.0 * sigma_next / half_width
        ) - sigma * sigma_next * previous
        previous = current
        current = following
        sigma = sigma_next
    return current


def solution(mesh):
    placed = (
        P(("row", "col"), None),
        P("row", "col", None, None, None),
        P("row", "col", None),
        P("row", "col", None),
        P(),
    )
    return jax.shard_map(
        local, mesh=mesh, in_specs=placed, out_specs=P(("row", "col"), None), check_vma=False
    )
```

profile of v0, /device:TPU:2, one launch (start us, length us, event | category | flops | bytes accessed | tf_op | source)
XLA Modules:
  0.0 1115.5 jit_solution(15374100512210820898)
XLA Ops:
  8.9 68.0 %all-gather.5.cloned.1.call-done = bf16[4096,256]{1,0:T(8,128)(2,1)} async-done(((bf16[128,256]{1,0:T(8,128)(2,1)}), bf16[4096,256]{1,0:T(8,128)(2,1)}) %all-gather.5.cloned.1.call-update) | async-done | bytes 2097168 | tf_op jit(solution)/shard_map/all_gather | solution.py:36
  76.9 2.2 gather_fusion
  79.6 1.7 copy.7
  81.4 1.7 pad.8
  86.5 33.2 %all_gather.25 = bf16[1024,256]{1,0:T(8,128)(2,1)S(1)} all-gather(bf16[128,256]{1,0:T(8,128)(2,1)S(1)} %copy-done.3), channel_id=1, replica_groups=mesh['row'=32,'col'=8] {'col'}, dimensions={0}, use_global_device_ids=true | all-gather | bytes 589824 | tf_op jit(solution)/shard_map/all_gather | solution.py:39
  120.8 1.7 copy.9
  122.5 1.7 pad.9
  125.4 3.8 fusion.35
  129.3 4.9 reshape.150
  138.5 24.8 %reduce-scatter.9.cloned.1.call-done = f32[128,256]{1,0:T(8,128)} async-done(((f32[1024,256]{1,0:T(8,128)}), f32[128,256]{1,0:T(8,128)}) %reduce-scatter.9.cloned.1.call-update) | async-done | bytes 131088 | tf_op jit(solution)/shard_map/reduce_scatter | solution.py:62
  163.3 124.4 %reduce-scatter.11.cloned.1.call-done = f32[128,256]{1,0:T(8,128)} async-done(((f32[4096,256]{1,0:T(8,128)}), f32[128,256]{1,0:T(8,128)}) %reduce-scatter.11.cloned.1.call-update) | async-done | bytes 131088 | tf_op jit(solution)/shard_map/reduce_scatter | solution.py:56
  287.7 1.6 fusion.58
  289.4 60.7 %all-gather.7.cloned.1.call-done = bf16[4096,256]{1,0:T(8,128)(2,1)} async-done(((bf16[128,256]{1,0:T(8,128)(2,1)}), bf16[4096,256]{1,0:T(8,128)(2,1)}) %all-gather.7.cloned.1.call-update) | async-done | bytes 2097168 | tf_op jit(solution)/shard_map/all_gather | solution.py:36
  350.1 2.2 gather_fusion.2
  352.8 1.7 copy.11
  354.5 1.7 pad.10
  359.6 33.3 %all_gather.27 = bf16[1024,256]{1,0:T(8,128)(2,1)S(1)} all-gather(bf16[128,256]{1,0:T(8,128)(2,1)S(1)} %copy-done.6), channel_id=1, replica_groups=mesh['row'=32,'col'=8] {'col'}, dimensions={0}, use_global_device_ids=true | all-gather | bytes 589824 | tf_op jit(solution)/shard_map/all_gather | solution.py:39
  394.1 1.7 copy.13
  395.8 1.7 pad.11
  398.8 3.8 fusion.34
  402.6 4.9 reshape.156
  407.7 29.0 %reduce-scatter.13.cloned.1.call-done = f32[128,256]{1,0:T(8,128)} async-done(((f32[1024,256]{1,0:T(8,128)}), f32[128,256]{1,0:T(8,128)}) %reduce-scatter.13.cloned.1.call-update) | async-done | bytes 131088 | tf_op jit(solution)/shard_map/reduce_scatter | solution.py:62
  436.6 124.1 %reduce-scatter.15.cloned.1.call-done = f32[128,256]{1,0:T(8,128)} async-done(((f32[4096,256]{1,0:T(8,128)}), f32[128,256]{1,0:T(8,128)}) %reduce-scatter.15.cloned.1.call-update) | async-done | bytes 131088 | tf_op jit(solution)/shard_map/reduce_scatter | solution.py:56
  560.7 1.6 fusion.57
  562.4 60.7 %all-gather.9.cloned.1.call-done = bf16[4096,256]{1,0:T(8,128)(2,1)} async-done(((bf16[128,256]{1,0:T(8,128)(2,1)}), bf16[4096,256]{1,0:T(8,128)(2,1)}) %all-gather.9.cloned.1.call-update) | async-done | bytes 2097168 | tf_op jit(solution)/shard_map/all_gather | solution.py:36
  623.1 2.2 gather_fusion.4
  625.8 1.7 copy.15
  627.6 1.7 pad.12
  632.6 33.5 %all_gather.29 = bf16[1024,256]{1,0:T(8,128)(2,1)S(1)} all-gather(bf16[128,256]{1,0:T(8,128)(2,1)S(1)} %copy-done.5), channel_id=1, replica_groups=mesh['row'=32,'col'=8] {'col'}, dimensions={0}, use_global_device_ids=true | all-gather | bytes 589824 | tf_op jit(solution)/shard_map/all_gather | solution.py:39
  667.3 1.7 copy.17
  669.0 1.7 pad.13
  672.0 3.8 fusion.33
  675.8 4.9 reshape.162
  680.8 28.9 %reduce-scatter.17.cloned.1.call-done = f32[128,256]{1,0:T(8,128)} async-done(((f32[1024,256]{1,0:T(8,128)}), f32[128,256]{1,0:T(8,128)}) %reduce-scatter.17.cloned.1.call-update) | async-done | bytes 131088 | tf_op jit(solution)/shard_map/reduce_scatter | solution.py:62
  709.7 124.3 %reduce-scatter.19.cloned.1.call-done = f32[128,256]{1,0:T(8,128)} async-done(((f32[4096,256]{1,0:T(8,128)}), f32[128,256]{1,0:T(8,128)}) %reduce-scatter.19.cloned.1.call-update) | async-done | bytes 131088 | tf_op jit(solution)/shard_map/reduce_scatter | solution.py:56
  834.0 1.7 fusion.56
  835.8 60.7 %all-gather.11.cloned.1.call-done = bf16[4096,256]{1,0:T(8,128)(2,1)} async-done(((bf16[128,256]{1,0:T(8,128)(2,1)}), bf16[4096,256]{1,0:T(8,128)(2,1)}) %all-gather.11.cloned.1.call-update) | async-done | bytes 2097168 | tf_op jit(solution)/shard_map/all_gather | solution.py:36
  896.4 2.2 gather_fusion.6
  899.2 1.7 copy.19
  900.9 1.7 pad.14
  906.0 33.6 %all_gather.31 = bf16[1024,256]{1,0:T(8,128)(2,1)S(1)} all-gather(bf16[128,256]{1,0:T(8,128)(2,1)S(1)} %copy-done.4), channel_id=1, replica_groups=mesh['row'=32,'col'=8] {'col'}, dimensions={0}, use_global_device_ids=true | all-gather | bytes 589824 | tf_op jit(solution)/shard_map/all_gather | solution.py:39
  940.7 1.7 copy.21
  942.4 1.7 pad.15
  945.3 3.8 fusion.32
  949.2 4.9 reshape.168
  954.1 28.8 %reduce-scatter.21.cloned.1.call-done = f32[128,256]{1,0:T(8,128)} async-done(((f32[1024,256]{1,0:T(8,128)}), f32[128,256]{1,0:T(8,128)}) %reduce-scatter.21.cloned.1.call-update) | async-done | bytes 131088 | tf_op jit(solution)/shard_map/reduce_scatter | solution.py:62
  982.9 124.0 %reduce-scatter.23.cloned.1.call-done = f32[128,256]{1,0:T(8,128)} async-done(((f32[4096,256]{1,0:T(8,128)}), f32[128,256]{1,0:T(8,128)}) %reduce-scatter.23.cloned.1.call-update) | async-done | bytes 131088 | tf_op jit(solution)/shard_map/reduce_scatter | solution.py:56
  1106.9 1.7 multiply_subtract_fusion
  (77 shorter events, 28.7 us)
Async XLA Ops:
  6.5 72.6 %copy-start = (bf16[1,1,14,128,128]{4,3,2,1,0:T(8,128)(2,1)S(1)}, bf16[1,1,14,128,128]{4,3,2,1,0:T(8,128)(2,1)}, u32[]{:S(2)}) copy-start(bf16[1,1,14,128,128]{4,3,2,1,0:T(8,128)(2,1)} %param.10) | copy-start | bytes 1376260
  6.5 70.4 %all-gather.5.cloned.1.call-start = ((), (), s32[]{:S(2)}) async-start(), calls=%async_computation.8 | async-start | bytes 2162688 | tf_op jit(solution)/shard_map/all_gather | solution.py:36
  8.2 155.2 %reduce-scatter.9.cloned.1.call-start = ((), (), s32[]{:S(2)}) async-start(), calls=%async_computation.9 | async-start | bytes 1179648 | tf_op jit(solution)/shard_map/reduce_scatter | solution.py:62
  85.1 1.3 copy-start.3
  86.4 201.3 %reduce-scatter.11.cloned.1.call-start = ((), (), s32[]{:S(2)}) async-start(), calls=%async_computation.10 | async-start | bytes 4325376 | tf_op jit(solution)/shard_map/reduce_scatter | solution.py:56
  134.1 0.7 copy-start.8
  134.1 153.6 %copy-start.1 = (f32[128,256]{1,0:T(8,128)S(1)}, f32[128,256]{1,0:T(8,128)}, u32[]{:S(2)}) copy-start(f32[128,256]{1,0:T(8,128)} %param.9) | copy-start | bytes 393220
  134.2 215.9 %all-gather.7.cloned.1.call-start = ((), (), s32[]{:S(2)}) async-start(), calls=%async_computation.11 | async-start | bytes 2162688 | tf_op jit(solution)/shard_map/all_gather | solution.py:36
  289.3 147.3 %reduce-scatter.13.cloned.1.call-start = ((), (), s32[]{:S(2)}) async-start(), calls=%async_computation.12 | async-start | bytes 1179648 | tf_op jit(solution)/shard_map/reduce_scatter | solution.py:62
  358.3 1.3 copy-start.6
  359.6 201.1 %reduce-scatter.15.cloned.1.call-start = ((), (), s32[]{:S(2)}) async-start(), calls=%async_computation.13 | async-start | bytes 4325376 | tf_op jit(solution)/shard_map/reduce_scatter | solution.py:56
  407.4 153.3 %copy-start.2 = (f32[128,256]{1,0:T(8,128)S(1)}, f32[128,256]{1,0:T(8,128)}, u32[]{:S(2)}) copy-start(f32[128,256]{1,0:T(8,128)} %param.9) | copy-start | bytes 393220
  407.5 215.7 %all-gather.9.cloned.1.call-start = ((), (), s32[]{:S(2)}) async-start(), calls=%async_computation.14 | async-start | bytes 2162688 | tf_op jit(solution)/shard_map/all_gather | solution.py:36
  562.4 147.3 %reduce-scatter.17.cloned.1.call-start = ((), (), s32[]{:S(2)}) async-start(), calls=%async_computation.15 | async-start | bytes 1179648 | tf_op jit(solution)/shard_map/reduce_scatter | solution.py:62
  631.3 1.3 copy-start.5
  632.6 201.4 %reduce-scatter.19.cloned.1.call-start = ((), (), s32[]{:S(2)}) async-start(), calls=%async_computation.16 | async-start | bytes 4325376 | tf_op jit(solution)/shard_map/reduce_scatter | solution.py:56
  680.7 215.8 %all-gather.11.cloned.1.call-start = ((), (), s32[]{:S(2)}) async-start(), calls=%async_computation.17 | async-start | bytes 2162688 | tf_op jit(solution)/shard_map/all_gather | solution.py:36
  835.7 147.2 %reduce-scatter.21.cloned.1.call-start = ((), (), s32[]{:S(2)}) async-start(), calls=%async_computation.18 | async-start | bytes 1179648 | tf_op jit(solution)/shard_map/reduce_scatter | solution.py:62
  904.6 1.3 copy-start.4
  905.9 201.0 %reduce-scatter.23.cloned.1.call-start = ((), (), s32[]{:S(2)}) async-start(), calls=%async_computation.19 | async-start | bytes 4325376 | tf_op jit(solution)/shard_map/reduce_scatter | solution.py:56
  954.0 152.9 %copy-start.7 = (f32[128,256]{1,0:T(8,128)S(1)}, f32[128,256]{1,0:T(8,128)}, u32[]{:S(2)}) copy-start(f32[128,256]{1,0:T(8,128)} %get-tuple-element.8) | copy-start | bytes 393220
Sparse Core Ops, SparseCore 0:
  9.2 67.6 all-gather.4
  86.5 76.7 reduce-scatter.8
  166.0 121.6 reduce-scatter.10
  289.6 60.4 all-gather.6
  359.7 76.9 reduce-scatter.12
  439.0 121.6 reduce-scatter.14
  562.6 60.5 all-gather.8
  632.7 76.9 reduce-scatter.16
  712.4 121.6 reduce-scatter.18
  835.9 60.5 all-gather.10
  906.0 76.8 reduce-scatter.20
  985.3 121.6 reduce-scatter.22
where the time goes:
time: 1120 us
  waiting for transfers between devices  858 us (77%)
  blocking collectives  134 us (12%)
  local copies, waits for them, and re-layouts  74.1 us (7%)
  matrix products  22.6 us (2%)
  between operations  17.4 us (2%)
    reduce_scatter x4, waiting for transfers between devices, apply_matrix(): lax.psum_scatter(far_partial.reshape(far_count * tile_size, vec_width), '...  497 us
    all_gather x4, waiting for transfers between devices, apply_matrix(): lax.all_gather(low_vectors, 'row', axis=0, tiled=True)  250 us
    all_gather x4, blocking collectives, apply_matrix(): lax.all_gather(low_vectors, 'col', axis=0, tiled=True)  134 us
    reduce_scatter x4, waiting for transfers between devices, apply_matrix(): lax.psum_scatter(near_partial.reshape(near_count * tile_size, vec_width),...  111 us
    unnamed x34, local copies, waits for them, and re-layouts  24 us
  transfers between devices with their start and end apart: 12, of which 12 were waited for; matrix products, arithmetic and copies ran while one was open for 5% of the time, Pallas kernels for 0%

commit v1 on v0

--- a/solution.py
+++ b/solution.py
@@ -4,6 +4,12 @@
 from jax.sharding import PartitionSpec as P
 
 DEGREE = 4
+
+
+def record_bring(x0, where_dim):
+    reached = jnp.stack([x0] * lax.axis_size("row"), axis=0)
+    piece_out = lax.all_to_all(reached, axis_name="row", split_axis=0, concat_axis=0)
+    return jnp.concatenate(piece_out, axis=where_dim)
 
 
 def local(start_block, tiles, tile_rows, tile_cols, bounds):
@@ -33,9 +39,7 @@
 
     def apply_matrix(vectors):
         low_vectors = vectors.astype(jnp.bfloat16)
-        far_vectors = lax.all_gather(low_vectors, "row", axis=0, tiled=True).reshape(
-            far_count, tile_size, vec_width
-        )
+        far_vectors = record_bring(low_vectors, 0).reshape(far_count, tile_size, vec_width)
         near_vectors = lax.all_gather(low_vectors, "col", axis=0, tiled=True).reshape(
             near_count, tile_size, vec_width
         )

time: 1120 us -> 1080 us (0.964)
  waiting for transfers between devices: 858 us -> 650 us
  blocking collectives: 134 us -> 295 us
    all_gather x4 -> x0, waiting for transfers between devices: 250 us -> none  [apply_matrix(): lax.all_gather(low_vectors, 'row', axis=0, tiled=True)]
    all_to_all x0 -> x3, blocking collectives: none -> 162 us  [record_bring(): lax.all_to_all(reached, axis_name='row', split_axis=0, concat_axis=0)]
    all_to_all x0 -> x1, waiting for transfers between devices: none -> 49.7 us  [record_bring(): lax.all_to_all(reached, axis_name='row', split_axis=0, concat_axis=0)]
    unnamed x34 -> x40, local copies, waits for them, and re-layouts: 24 us -> 24 us
  transfers between devices with their start and end apart: 12 -> 9, of which waited for: 12 -> 9; matrix products, arithmetic and copies ran while one was open for 5% -> 6% of each run, Pallas kernels for 0% -> 0%
where the time goes in v1:
time: 1080 us; the launch traced here: 1070 us
  waiting for transfers between devices  650 us (60%)
  blocking collectives  295 us (27%)
  local copies, waits for them, and re-layouts  70.9 us (7%)
  matrix products  22.4 us (2%)
  between operations  17.5 us (2%)
    reduce_scatter x4, waiting for transfers between devices, apply_matrix(): lax.psum_scatter(far_partial.reshape(far_count * tile_size, vec_width), '...  497 us
    all_to_all x3, blocking collectives, record_bring(): lax.all_to_all(reached, axis_name='row', split_axis=0, concat_axis=0)  162 us
    all_gather x4, blocking collectives, apply_matrix(): lax.all_gather(low_vectors, 'col', axis=0, tiled=True)  134 us
    reduce_scatter x4, waiting for transfers between devices, apply_matrix(): lax.psum_scatter(near_partial.reshape(near_count * tile_size, vec_width),...  103 us
    all_to_all x1, waiting for transfers between devices, record_bring(): lax.all_to_all(reached, axis_name='row', split_axis=0, concat_axis=0)  49.7 us
    unnamed x40, local copies, waits for them, and re-layouts  24 us
  transfers between devices with their start and end apart: 9, of which 9 were waited for; matrix products, arithmetic and copies ran while one was open for 6% of the time, Pallas kernels for 0%

profile of v1, /device:TPU:2, one launch (start us, length us, event | category | flops | bytes accessed | tf_op | source)
XLA Modules:
  0.0 1074.3 jit_solution(9172764070397076197)
XLA Ops:
  7.5 1.6 stack.8
  9.1 10.0 all-to-all-start
  19.8 49.7 %all-to-all-done = bf16[32,128,256]{2,1,0:T(8,128)(2,1)S(1)} async-done(((bf16[32,128,256]{2,1,0:T(8,128)(2,1)}), bf16[32,128,256]{2,1,0:T(8,128)(2,1)S(1)}, u32[]{:S(2)}, u32[]{:S(2)}) %all-to-all-start) | async-done | bytes 2097184 | tf_op jit(solution)/shard_map/all_to_all | solution.py:11
  70.8 1.7 copy.7
  72.5 1.7 pad.8
  76.3 1.2 reshape.142
  77.6 33.1 %all_gather.12 = bf16[1024,256]{1,0:T(8,128)(2,1)S(1)} all-gather(bf16[128,256]{1,0:T(8,128)(2,1)S(1)} %convert_element_type.14), channel_id=1, replica_groups=mesh['row'=32,'col'=8] {'col'}, dimensions={0}, use_global_device_ids=true | all-gather | bytes 589824 | tf_op jit(solution)/shard_map/all_gather | solution.py:43
  111.8 1.7 copy.9
  113.5 1.7 pad.9
  116.5 3.8 fusion.35
  120.2 4.9 reshape.145
  129.7 23.5 %reduce-scatter.9.cloned.1.call-done = f32[128,256]{1,0:T(8,128)} async-done(((f32[1024,256]{1,0:T(8,128)}), f32[128,256]{1,0:T(8,128)}) %reduce-scatter.9.cloned.1.call-update) | async-done | bytes 131088 | tf_op jit(solution)/shard_map/reduce_scatter | solution.py:66
  153.2 124.4 %reduce-scatter.11.cloned.1.call-done = f32[128,256]{1,0:T(8,128)} async-done(((f32[4096,256]{1,0:T(8,128)}), f32[128,256]{1,0:T(8,128)}) %reduce-scatter.11.cloned.1.call-update) | async-done | bytes 131088 | tf_op jit(solution)/shard_map/reduce_scatter | solution.py:60
  277.6 1.7 fusion.58
  279.4 53.9 %all_to_all.20 = bf16[32,128,256]{2,1,0:T(8,128)(2,1)S(1)} all-to-all(bf16[32,128,256]{2,1,0:T(8,128)(2,1)S(1)} %stack.9), channel_id=1, replica_groups=mesh['row'=32,'col'=8] {'row'}, dimensions={0} | all-to-all | bytes 4194304 | tf_op jit(solution)/shard_map/all_to_all | solution.py:11
  334.6 1.7 copy.11
  336.3 1.7 pad.10
  340.0 1.2 reshape.147
  341.3 33.4 %all_gather.13 = bf16[1024,256]{1,0:T(8,128)(2,1)S(1)} all-gather(bf16[128,256]{1,0:T(8,128)(2,1)S(1)} %get-tuple-element.11), channel_id=1, replica_groups=mesh['row'=32,'col'=8] {'col'}, dimensions={0}, use_global_device_ids=true | all-gather | bytes 589824 | tf_op jit(solution)/shard_map/all_gather | solution.py:43
  376.0 1.7 copy.13
  377.7 1.7 pad.11
  380.7 3.8 fusion.34
  384.4 4.9 reshape.150
  389.6 26.4 %reduce-scatter.13.cloned.1.call-done = f32[128,256]{1,0:T(8,128)} async-done(((f32[1024,256]{1,0:T(8,128)}), f32[128,256]{1,0:T(8,128)}) %reduce-scatter.13.cloned.1.call-update) | async-done | bytes 131088 | tf_op jit(solution)/shard_map/reduce_scatter | solution.py:66
  416.0 124.1 %reduce-scatter.15.cloned.1.call-done = f32[128,256]{1,0:T(8,128)} async-done(((f32[4096,256]{1,0:T(8,128)}), f32[128,256]{1,0:T(8,128)}) %reduce-scatter.15.cloned.1.call-update) | async-done | bytes 131088 | tf_op jit(solution)/shard_map/reduce_scatter | solution.py:60
  540.1 1.6 fusion.57
  542.0 53.9 %all_to_all.21 = bf16[32,128,256]{2,1,0:T(8,128)(2,1)S(1)} all-to-all(bf16[32,128,256]{2,1,0:T(8,128)(2,1)S(1)} %stack.10), channel_id=1, replica_groups=mesh['row'=32,'col'=8] {'row'}, dimensions={0} | all-to-all | bytes 4194304 | tf_op jit(solution)/shard_map/all_to_all | solution.py:11
  597.1 1.7 copy.15
  598.8 1.7 pad.12
  603.8 33.6 %all_gather.14 = bf16[1024,256]{1,0:T(8,128)(2,1)S(1)} all-gather(bf16[128,256]{1,0:T(8,128)(2,1)S(1)} %get-tuple-element.9), channel_id=1, replica_groups=mesh['row'=32,'col'=8] {'col'}, dimensions={0}, use_global_device_ids=true | all-gather | bytes 589824 | tf_op jit(solution)/shard_map/all_gather | solution.py:43
  638.7 1.7 copy.17
  640.5 1.7 pad.13
  643.4 3.8 fusion.33
  647.2 4.9 reshape.155
  652.2 26.5 %reduce-scatter.17.cloned.1.call-done = f32[128,256]{1,0:T(8,128)} async-done(((f32[1024,256]{1,0:T(8,128)}), f32[128,256]{1,0:T(8,128)}) %reduce-scatter.17.cloned.1.call-update) | async-done | bytes 131088 | tf_op jit(solution)/shard_map/reduce_scatter | solution.py:66
  678.8 124.2 %reduce-scatter.19.cloned.1.call-done = f32[128,256]{1,0:T(8,128)} async-done(((f32[4096,256]{1,0:T(8,128)}), f32[128,256]{1,0:T(8,128)}) %reduce-scatter.19.cloned.1.call-update) | async-done | bytes 131088 | tf_op jit(solution)/shard_map/reduce_scatter | solution.py:60
  803.0 1.7 fusion.56
  804.9 53.9 %all_to_all.22 = bf16[32,128,256]{2,1,0:T(8,128)(2,1)S(1)} all-to-all(bf16[32,128,256]{2,1,0:T(8,128)(2,1)S(1)} %stack.11), channel_id=1, replica_groups=mesh['row'=32,'col'=8] {'row'}, dimensions={0} | all-to-all | bytes 4194304 | tf_op jit(solution)/shard_map/all_to_all | solution.py:11
  860.0 1.7 copy.19
  861.7 1.7 pad.14
  866.8 33.6 %all_gather.15 = bf16[1024,256]{1,0:T(8,128)(2,1)S(1)} all-gather(bf16[128,256]{1,0:T(8,128)(2,1)S(1)} %get-tuple-element.6), channel_id=1, replica_groups=mesh['row'=32,'col'=8] {'col'}, dimensions={0}, use_global_device_ids=true | all-gather | bytes 589824 | tf_op jit(solution)/shard_map/all_gather | solution.py:43
  901.6 1.7 copy.21
  903.4 1.7 pad.15
  906.3 3.8 fusion.32
  910.1 4.9 reshape.160
  915.1 26.6 %reduce-scatter.21.cloned.1.call-done = f32[128,256]{1,0:T(8,128)} async-done(((f32[1024,256]{1,0:T(8,128)}), f32[128,256]{1,0:T(8,128)}) %reduce-scatter.21.cloned.1.call-update) | async-done | bytes 131088 | tf_op jit(solution)/shard_map/reduce_scatter | solution.py:66
  941.7 124.2 %reduce-scatter.23.cloned.1.call-done = f32[128,256]{1,0:T(8,128)} async-done(((f32[4096,256]{1,0:T(8,128)}), f32[128,256]{1,0:T(8,128)}) %reduce-scatter.23.cloned.1.call-update) | async-done | bytes 131088 | tf_op jit(solution)/shard_map/reduce_scatter | solution.py:60
  1065.8 1.7 multiply_subtract_fusion
  (80 shorter events, 29.2 us)
Async XLA Ops:
  6.5 63.7 %copy-start = (bf16[1,1,14,128,128]{4,3,2,1,0:T(8,128)(2,1)S(1)}, bf16[1,1,14,128,128]{4,3,2,1,0:T(8,128)(2,1)}, u32[]{:S(2)}) copy-start(bf16[1,1,14,128,128]{4,3,2,1,0:T(8,128)(2,1)} %param.10) | copy-start | bytes 1376260
  9.1 10.1 copy-start.10
  9.1 10.1 copy-start.11
  9.1 60.4 %all-to-all-start = ((bf16[32,128,256]{2,1,0:T(8,128)(2,1)}), bf16[32,128,256]{2,1,0:T(8,128)(2,1)S(1)}, u32[]{:S(2)}, u32[]{:S(2)}) async-start(bf16[32,128,256]{2,1,0:T(8,128)(2,1)} %stack.8), calls=%async_computation | async-start | bytes 4194304 | tf_op jit(solution)/shard_map/all_to_all | solution.py:11
  19.1 134.1 %reduce-scatter.9.cloned.1.call-start = ((), (), s32[]{:S(2)}) async-start(), calls=%async_computation.12 | async-start | bytes 1179648 | tf_op jit(solution)/shard_map/reduce_scatter | solution.py:66
  77.5 200.1 %reduce-scatter.11.cloned.1.call-start = ((), (), s32[]{:S(2)}) async-start(), calls=%async_computation.13 | async-start | bytes 4325376 | tf_op jit(solution)/shard_map/reduce_scatter | solution.py:60
  77.6 34.2 %copy-start.8 = (s32[1024]{0:T(1024)}, s32[1024]{0:T(1024)S(1)}, u32[]{:S(2)}) copy-start(s32[1024]{0:T(1024)S(1)} %pad_clamp_fusion) | copy-start | bytes 12292
  125.1 0.7 copy-start.9
  125.1 152.4 %copy-start.5 = (f32[128,256]{1,0:T(8,128)S(1)}, f32[128,256]{1,0:T(8,128)}, u32[]{:S(2)}) copy-start(f32[128,256]{1,0:T(8,128)} %param.9) | copy-start | bytes 393220
  125.2 290.8 %reduce-scatter.13.cloned.1.call-start = ((), (), s32[]{:S(2)}) async-start(), calls=%async_computation.14 | async-start | bytes 1179648 | tf_op jit(solution)/shard_map/reduce_scatter | solution.py:66
  341.3 198.8 %reduce-scatter.15.cloned.1.call-start = ((), (), s32[]{:S(2)}) async-start(), calls=%async_computation.15 | async-start | bytes 4325376 | tf_op jit(solution)/shard_map/reduce_scatter | solution.py:60
  389.3 150.7 %copy-start.3 = (f32[128,256]{1,0:T(8,128)S(1)}, f32[128,256]{1,0:T(8,128)}, u32[]{:S(2)}) copy-start(f32[128,256]{1,0:T(8,128)} %get-tuple-element.12) | copy-start | bytes 393220
  389.3 150.7 %copy-start.6 = (f32[128,256]{1,0:T(8,128)S(1)}, f32[128,256]{1,0:T(8,128)}, u32[]{:S(2)}) copy-start(f32[128,256]{1,0:T(8,128)} %param.9) | copy-start | bytes 393220
  389.4 289.4 %reduce-scatter.17.cloned.1.call-start = ((), (), s32[]{:S(2)}) async-start(), calls=%async_computation.16 | async-start | bytes 1179648 | tf_op jit(solution)/shard_map/reduce_scatter | solution.py:66
  603.8 199.2 %reduce-scatter.19.cloned.1.call-start = ((), (), s32[]{:S(2)}) async-start(), calls=%async_computation.17 | async-start | bytes 4325376 | tf_op jit(solution)/shard_map/reduce_scatter | solution.py:60
  652.1 150.9 %copy-start.1 = (f32[128,256]{1,0:T(8,128)S(1)}, f32[128,256]{1,0:T(8,128)}, u32[]{:S(2)}) copy-start(f32[128,256]{1,0:T(8,128)} %get-tuple-element.10) | copy-start | bytes 393220
  652.1 150.9 %copy-start.4 = (f32[128,256]{1,0:T(8,128)S(1)}, f32[128,256]{1,0:T(8,128)}, u32[]{:S(2)}) copy-start(f32[128,256]{1,0:T(8,128)} %get-tuple-element.12) | copy-start | bytes 393220
  652.1 289.6 %reduce-scatter.21.cloned.1.call-start = ((), (), s32[]{:S(2)}) async-start(), calls=%async_computation.18 | async-start | bytes 1179648 | tf_op jit(solution)/shard_map/reduce_scatter | solution.py:66
  866.7 199.1 %reduce-scatter.23.cloned.1.call-start = ((), (), s32[]{:S(2)}) async-start(), calls=%async_computation.19 | async-start | bytes 4325376 | tf_op jit(solution)/shard_map/reduce_scatter | solution.py:60
  915.0 150.9 %copy-start.2 = (f32[128,256]{1,0:T(8,128)S(1)}, f32[128,256]{1,0:T(8,128)}, u32[]{:S(2)}) copy-start(f32[128,256]{1,0:T(8,128)} %get-tuple-element.10) | copy-start | bytes 393220
  915.0 150.9 %copy-start.7 = (f32[128,256]{1,0:T(8,128)S(1)}, f32[128,256]{1,0:T(8,128)}, u32[]{:S(2)}) copy-start(f32[128,256]{1,0:T(8,128)} %get-tuple-element.8) | copy-start | bytes 393220
Sparse Core Ops, SparseCore 0:
  77.6 75.4 reduce-scatter.8
  155.9 121.6 reduce-scatter.10
  341.4 74.5 reduce-scatter.12
  418.4 121.6 reduce-scatter.14
  603.9 74.7 reduce-scatter.16
  681.3 121.6 reduce-scatter.18
  866.8 74.7 reduce-scatter.20
  944.2 121.6 reduce-scatter.22
